TPU v7x, 128 devices: a whole 4x4x4 slice. The times are simulated.
128 devices in a mesh: node: 4 (over x), local: 32 (over y, z, core).
Axes of the slice: x: 4, y: 4, z: 4, core: 2. Of those that a mesh axis runs over, the one named last changes fastest.
Arguments:
- tokens: bfloat16 [16384, 7168], P(('node', 'local')), may hold values from -6 to 6
- expert_ids: int32 [16384, 8], P(('node', 'local')), may hold values from 0 to 255, all different within a row; in each aligned block of 128 rows (0 to 127, 128 to 255, ...) at most 5 rows name the same one
- route_weights: float32 [16384, 8], P(('node', 'local')), may hold values from 0.1 to 1
- grad_out: bfloat16 [16384, 7168], P(('node', 'local')), may hold values from -1.5 to 1.5
- gate_weight: bfloat16 [7168, 16384], P(None, ('node', 'local')), may hold values from -0.0625 to 0.0625
- up_weight: bfloat16 [7168, 16384], P(None, ('node', 'local')), may hold values from -0.0625 to 0.0625
- down_weight: bfloat16 [16384, 7168], P(('node', 'local')), may hold values from -0.1875 to 0.1875
Outputs:
- mixed: bfloat16 [16384, 7168], P(('node', 'local'))
- grad_tokens: bfloat16 [16384, 7168], P(('node', 'local'))
- grad_weights: float32 [16384, 8], P(('node', 'local'))
- grad_gate: bfloat16 [7168, 16384], P(None, ('node', 'local'))
- grad_up: bfloat16 [7168, 16384], P(None, ('node', 'local'))
- grad_down: bfloat16 [16384, 7168], P(('node', 'local'))
Inputs may be any that keep to these rules, and one draw needn't show every extreme that they name: `expert_ids`: A row names 8 different ids. In the 128 rows of one device no id is named by more than 5 rows, a bound that some block reaches.
All inputs are finite; a program needn't handle non-finite values. Where the computation divides by a largest or mean magnitude, that divisor is 1e-20 or more.
Results may differ from a plain program's by a relative error of at most 0.012.
Values may be sent and summed in bfloat16 or wider, within the bound.
A program may use at most 192 MiB of HBM per device.

v0:
```python
import functools

import jax
import jax.numpy as jnp
from jax import lax
from jax.experimental import pallas as pl
from jax.experimental.pallas import tpu as pltpu
from jax.sharding import PartitionSpec as P

F32 = jnp.float32
BF16 = jnp.bfloat16
MESH = pl.DeviceIdType.MESH

TOKENS = 128
TOP = 8
D = 7168
HID = 128
NX, NY, NZ = 4, 4, 4
EXPERTS = NX * NY
CAP = 5
PAD = 16
SEGS = 3
PACK = EXPERTS * PAD
HALF = EXPERTS * CAP
BLOCK = 2 * HALF
GROUP = NZ * BLOCK
ROWS = 2 * NZ * HALF
CW = 512
NQ = D // CW
NF = NQ // 2
AHEAD = 2
PAIR = 2 * CW
SEG = 384
BACK = 12
GRADS = NQ + 3
PARTS = 4
VMEM_LIMIT = 64 * 1024 * 1024 - 1024 * 1024


def dot(a, b):
    return jnp.dot(a, b, preferred_element_type=F32)


def dot_nt(a, b):
    return lax.dot_general(a, b, (((1,), (1,)), ((), ())), preferred_element_type=F32)


def kernel(
    ids_hbm,
    weights_hbm,
    tokens_hbm,
    cot_hbm,
    gate_hbm,
    up_hbm,
    down_hbm,
    mixed_hbm,
    dtok_hbm,
    dw_hbm,
    dgate_hbm,
    dup_hbm,
    ddown_hbm,
    pack,
    inbox,
    partial,
    gathered,
    wide,
    down,
    cot,
    sums,
    other,
    ring_lo,
    ring_hi,
    far_lo,
    far_hi,
    back,
    st_fin,
    st_down,
    st_wide,
    ids_ref,
    weights_ref,
    dw_ref,
    chosen,
    select,
    finish,
    compact,
    expand,
    row_scale,
    pre,
    dhid,
    hid,
    dpre,
    hid_t,
    dpre_t,
    scores,
    load_sem,
    fs,
    fr,
    ags,
    ag_other,
    ag_lo,
    ag_hi,
    ag_far_lo,
    ag_far_hi,
    ps,
    pr,
    ss,
    rr_lo,
    rr_hi,
    rr_far_lo,
    rr_far_hi,
    ts,
    tr,
    fin_sem,
    grad_sem,
):
    x = lax.axis_index("node")
    local = lax.axis_index("local")
    y = local // (2 * NZ)
    z = (local // 2) % NZ
    c = local % 2
    z_up, z_dn, z_far = (z + 1) % NZ, (z + NZ - 1) % NZ, (z + 2) % NZ
    here = x * NY + y
    me = c * NZ + z
    partner = (x, y * 2 * NZ + z * 2 + (1 - c))
    up = (x, y * 2 * NZ + z_up * 2 + c)
    dn = (x, y * 2 * NZ + z_dn * 2 + c)

    def peer(k):
        px = (x + k // NY) % NX
        py = (y + k % NY) % NY
        return px * NY + py, (px, py * 2 * NZ + z * 2 + c)

    def cols_of(q):
        return pl.ds(pl.multiple_of(q * CW, CW), CW)

    def pair_of(q):
        return pl.ds(pl.multiple_of(q * PAIR, PAIR), PAIR)

    def token_rows(q):
        return pl.ds(pl.multiple_of(q * TOKENS, TOKENS), TOKENS)

    def token_copy(q):
        return pltpu.make_async_copy(tokens_hbm.at[:, cols_of(q)], sums.at[token_rows(q)], load_sem.at[0, q])

    def cot_copy(q):
        return pltpu.make_async_copy(cot_hbm.at[:, pair_of(q)], cot.at[q], load_sem.at[1, q])

    def down_copy(q):
        return pltpu.make_async_copy(down_hbm.at[:, cols_of(q)], down.at[q], load_sem.at[2, q])

    ids_copy = pltpu.make_async_copy(ids_hbm, ids_ref, load_sem.at[3, 0])
    weights_copy = pltpu.make_async_copy(weights_hbm, weights_ref, load_sem.at[3, 1])
    gate_copy = pltpu.make_async_copy(gate_hbm, wide.at[:, pl.ds(0, HID)], load_sem.at[3, 2])
    up_copy = pltpu.make_async_copy(up_hbm, wide.at[:, pl.ds(HID, HID)], load_sem.at[3, 3])
    ids_copy.start()
    weights_copy.start()

    @pl.loop(0, NQ)
    def _(q):
        token_copy(q).start()

    gate_copy.start()
    up_copy.start()

    @pl.loop(0, NF)
    def _(q):
        cot_copy(q).start()
        down_copy(2 * q).start()
        down_copy(2 * q + 1).start()

    barrier = pltpu.get_barrier_semaphore()

    @pl.loop(1, EXPERTS)
    def _(k):
        _, device = peer(k)
        pl.semaphore_signal(barrier, inc=1, device_id=device, device_id_type=MESH)

    for device in (partner, up, dn):
        pl.semaphore_signal(barrier, inc=1, device_id=device, device_id_type=MESH)

    ids_copy.wait()
    weights_copy.wait()
    row = lax.broadcasted_iota(jnp.int32, (PACK, TOKENS), 0)
    expert, place = row // PAD, row % PAD
    segment = place // CAP
    rank_of = jnp.where(segment < SEGS, place % CAP, -1).astype(F32)
    named = jnp.zeros((PACK, TOKENS), F32)
    weight_of = jnp.zeros((PACK, TOKENS), F32)
    for k in range(TOP):
        hit = ids_ref[k : k + 1, :] == expert
        named = jnp.where(hit, 1.0, named)
        weight_of = jnp.where(hit, weights_ref[k : k + 1, :], weight_of)
    earlier = lax.broadcasted_iota(jnp.int32, (TOKENS, TOKENS), 0) < lax.broadcasted_iota(
        jnp.int32, (TOKENS, TOKENS), 1
    )
    rank = dot(named.astype(BF16), jnp.where(earlier, 1.0, 0.0).astype(BF16))
    picks = jnp.where((named > 0.5) & (rank == rank_of), 1.0, 0.0)
    chosen[...] = picks
    for k in range(SEGS):
        select[:, pl.ds(k * TOKENS, TOKENS)] = jnp.where(segment == k, picks, 0.0).astype(BF16)
    row_scale[...] = jnp.broadcast_to(jnp.sum(picks * weight_of, axis=1, keepdims=True), (PACK, 128))

    def slot_target(shape, dim):
        r = lax.broadcasted_iota(jnp.int32, shape, dim)
        e, i = r // PAD, r % PAD
        return jnp.where(i < SEGS * CAP, (i // CAP) * HALF + e * CAP + i % CAP, -1)

    def send_packets(q, dst_at, send_sem, recv_sem):
        pltpu.make_async_copy(
            pack.at[q, pl.ds(pl.multiple_of(here * PAD, PAD), PAD)], dst_at(q, here), recv_sem
        ).start()

        @pl.loop(1, EXPERTS)
        def _(k):
            e, device = peer(k)
            pltpu.make_async_remote_copy(
                src_ref=pack.at[q, pl.ds(pl.multiple_of(e * PAD, PAD), PAD)],
                dst_ref=dst_at(q, here),
                send_sem=send_sem.at[q],
                recv_sem=recv_sem,
                device_id=device,
                device_id_type=MESH,
            ).start()

    def inbox_at(q, e):
        return inbox.at[q, pl.ds(pl.multiple_of(e * PAD, PAD), PAD)]

    def back_at(q, e):
        return back.at[q, pl.ds(pl.multiple_of(e * PAD, PAD), PAD)]

    def wait_bytes(ref, sem):
        pltpu.make_async_copy(ref, ref, sem).wait()

    def wait_packet_sends(q, send_sem):
        wait_bytes(pack.at[q, pl.ds(0, PACK - PAD)], send_sem.at[q])

    def decode(q):
        token_copy(q).wait()
        values = sums[token_rows(q), :].astype(F32)
        parts = []
        for b in range(CW // 128):
            v = values[:, b * 128 : (b + 1) * 128]
            scale = (jnp.max(jnp.abs(v), axis=1, keepdims=True) + 1e-06).astype(BF16).astype(F32)
            code = (v / scale).astype(BF16).astype(F32)
            parts.append((code * scale).astype(BF16))
        return parts

    def segments(rows):
        short = rows[:, 2 * SEG :]
        zeros = jnp.zeros((rows.shape[0], SEGS * SEG - PAIR), BF16)
        return jnp.concatenate([rows[:, :SEG], rows[:, SEG : 2 * SEG], jnp.concatenate([short, zeros], axis=1)], axis=0)

    def prepare(q):
        @pl.when(q < NF)
        def _():
            decoded = jnp.concatenate(decode(2 * q) + decode(2 * q + 1), axis=1)
            pack[q] = dot(select[...], segments(decoded)).astype(BF16)

        @pl.when(q >= NF)
        def _():
            cot_copy(q - NF).wait()
            pack[q] = (dot(select[...], segments(cot[q - NF])) * row_scale[:, 0:1]).astype(BF16)

    def send_forward(q):
        send_packets(q, inbox_at, fs, fr.at[q])

    def remote(src, dst, send_sem, recv_sem, device):
        pltpu.make_async_remote_copy(
            src_ref=src, dst_ref=dst, send_sem=send_sem, recv_sem=recv_sem, device_id=device, device_id_type=MESH
        ).start()

    lower, upper = pl.ds(0, HALF), pl.ds(HALF, HALF)

    def activate():
        @pl.loop(0, ROWS // HID)
        def _(i):
            rows = pl.ds(pl.multiple_of(i * HID, HID), HID)
            gate_pre = pre[rows, 0:HID]
            sig = 1.0 / (1.0 + jnp.exp(-gate_pre))
            hid[rows, :] = (gate_pre * sig * pre[rows, HID : 2 * HID]).astype(BF16)

        for i in range(ROWS // HID):
            rows = slice(i * HID, (i + 1) * HID)
            hid_t[:, rows] = hid[rows, :].astype(F32).T.astype(BF16)

    def activate_back():
        @pl.loop(0, ROWS // HID)
        def _(i):
            rows = pl.ds(pl.multiple_of(i * HID, HID), HID)
            gate_pre = pre[rows, 0:HID]
            grad_hidden = dhid[rows, :]
            sig = 1.0 / (1.0 + jnp.exp(-gate_pre))
            slope = sig * (1.0 + gate_pre * (1.0 - sig))
            dpre[rows, 0:HID] = (grad_hidden * pre[rows, HID : 2 * HID] * slope).astype(BF16)
            dpre[rows, HID : 2 * HID] = (grad_hidden * (gate_pre * sig)).astype(BF16)

        for i in range(ROWS // HID):
            rows = slice(i * HID, (i + 1) * HID)
            dpre_t[0:HID, rows] = dpre[rows, 0:HID].astype(F32).T.astype(BF16)
            dpre_t[HID : 2 * HID, rows] = dpre[rows, HID : 2 * HID].astype(F32).T.astype(BF16)

    def partial_rows(q, side, zz, size=BLOCK, offset=0):
        start = (q % 2) * 2 * GROUP + side * GROUP + zz * BLOCK + offset
        return pl.ds(pl.multiple_of(start, PAD), size)

    def other_rows(zz, size=BLOCK, offset=0):
        return pl.ds(pl.multiple_of(zz * BLOCK + offset, PAD), size)

    def sum_rows(q, k, size=BLOCK, offset=0):
        return pl.ds(pl.multiple_of((q % 4) * GROUP + k * BLOCK + offset, PAD), size)

    def grad_copies(q):
        slot = q % 2
        rows = cols_of(q)
        return (
            pltpu.make_async_copy(st_down.at[slot], ddown_hbm.at[:, rows], grad_sem.at[0, slot]),
            pltpu.make_async_copy(st_wide.at[slot, :, pl.ds(0, HID)], dgate_hbm.at[rows], grad_sem.at[1, slot]),
            pltpu.make_async_copy(st_wide.at[slot, :, pl.ds(HID, HID)], dup_hbm.at[rows], grad_sem.at[2, slot]),
        )

    def fin_copy(q, out_hbm):
        slot = q % 2
        return pltpu.make_async_copy(st_fin.at[slot], out_hbm.at[:, pair_of(q % NF)], fin_sem.at[slot])

    def pair_sum(q, zz, size, offset):
        mine = partial[partial_rows(q, c, zz, size, offset), :].astype(F32)
        return mine + other[q, other_rows(zz, size, offset), :].astype(F32)

    dw_copy = pltpu.make_async_copy(dw_ref, dw_hbm, load_sem.at[3, 0])

    def keep_own(q):
        wait_bytes(inbox.at[q], fr.at[q])
        kept = dot(compact[...], inbox[q]).astype(BF16)
        gathered[q, me, 0:HALF, 0:SEG] = kept[0:HALF]
        gathered[q, me, 0:HALF, SEG:CW] = kept[HALF : 2 * HALF, 0 : CW - SEG]
        gathered[q, me, HALF:BLOCK, 0 : 2 * SEG - CW] = kept[HALF : 2 * HALF, CW - SEG : SEG]
        gathered[q, me, HALF:BLOCK, 2 * SEG - CW : CW] = kept[2 * HALF :, 0 : PAIR - 2 * SEG]
        mine = gathered.at[q, me]
        remote(mine, mine, ags.at[q], ag_lo.at[q], up)
        remote(mine, mine, ags.at[q], ag_hi.at[q], dn)
        remote(mine, mine, ags.at[q], ag_other.at[q], partner)

    prepare(0)
    pl.semaphore_wait(barrier, EXPERTS - 1 + 3)
    send_forward(0)
    compact[...] = jnp.where(
        lax.broadcasted_iota(jnp.int32, (SEGS * HALF, PACK), 0) == slot_target((SEGS * HALF, PACK), 1), 1.0, 0.0
    ).astype(BF16)
    prepare(1)
    send_forward(1)
    keep_own(0)
    prepare(2)
    send_forward(2)
    for k in range(SEGS):
        finish[pl.ds(k * TOKENS, TOKENS), :] = jnp.where(segment == k, chosen[...], 0.0).T.astype(BF16)
    expand[...] = jnp.where(
        lax.broadcasted_iota(jnp.int32, (PACK, SEGS * HALF), 1) == slot_target((PACK, SEGS * HALF), 0), 1.0, 0.0
    ).astype(BF16)
    pre[...] = jnp.zeros_like(pre)
    dhid[...] = jnp.zeros_like(dhid)
    scores[...] = jnp.zeros_like(scores)

    @pl.loop(1, BACK + NQ + 4)
    def _(t):
        r = t - BACK

        @pl.when(t < NQ)
        def _():
            keep_own(t)

        @pl.when((t >= 1) & (t < NQ + 1))
        def _():
            q = t - 1
            from_lo = gathered.at[q, c * NZ + z_dn]
            wait_bytes(from_lo, ag_lo.at[q])
            half = gathered.at[q, c * NZ + z_dn, lower]
            remote(half, half, ags.at[q], ag_far_lo.at[q], up)
            remote(from_lo, from_lo, ags.at[q], ag_other.at[q], partner)
            from_hi = gathered.at[q, c * NZ + z_up]
            wait_bytes(from_hi, ag_hi.at[q])
            half = gathered.at[q, c * NZ + z_up, upper]
            remote(half, half, ags.at[q], ag_far_hi.at[q], dn)
            remote(from_hi, from_hi, ags.at[q], ag_other.at[q], partner)

        @pl.when(t + AHEAD < NQ)
        def _():
            prepare(t + AHEAD)
            send_forward(t + AHEAD)

        @pl.when((t >= 2) & (t < NQ + 2))
        def _():
            q = t - 2
            half = gathered.at[q, c * NZ + z_far, lower]
            wait_bytes(half, ag_far_lo.at[q])
            remote(half, half, ags.at[q], ag_other.at[q], partner)
            half = gathered.at[q, c * NZ + z_far, upper]
            wait_bytes(half, ag_far_hi.at[q])
            remote(half, half, ags.at[q], ag_other.at[q], partner)

        @pl.when(t == 3)
        def _():
            gate_copy.wait()
            up_copy.wait()

        @pl.when((t >= 3) & (t < NQ + 3))
        def _():
            q = t - 3
            theirs = gathered.at[q, pl.ds((1 - c) * NZ, NZ)]
            wait_bytes(theirs, ag_other.at[q])
            rows_even = gathered[q, :, 0:HALF, :].reshape(ROWS, CW)
            rows_odd = gathered[q, :, HALF:BLOCK, :].reshape(ROWS, CW)

            @pl.when(q < NF)
            def _():
                pre[...] += dot(rows_even, wide[cols_of(2 * q), :]) + dot(rows_odd, wide[cols_of(2 * q + 1), :])

            @pl.when(q >= NF)
            def _():
                k = q - NF
                down_copy(2 * k).wait()
                down_copy(2 * k + 1).wait()
                dhid[...] += dot_nt(rows_even, down[2 * k]) + dot_nt(rows_odd, down[2 * k + 1])

            pl.when(q == NF - 1)(activate)
            pl.when(q == NQ - 1)(activate_back)

        @pl.when((r >= 0) & (r < NQ))
        def _():
            q = r

            @pl.when(q >= 2)
            def _():
                wait_bytes(other.at[q - 2], ps.at[q - 2])

            def keep(parts):
                for j in range(2 * NZ):
                    for h in range(2):
                        base = (q % 2) * 2 * GROUP + j * BLOCK + h * HALF
                        partial[pl.ds(pl.multiple_of(base, PAD), HALF), :] = parts[h][j * HALF : (j + 1) * HALF]

            @pl.when(q < NF)
            def _():
                keep([dot(hid[...], down[2 * q + h]).astype(BF16) for h in range(2)])

            @pl.when(q >= NF)
            def _():
                keep([dot_nt(dpre[...], wide[cols_of(2 * (q - NF) + h), :]).astype(BF16) for h in range(2)])

            remote(partial.at[partial_rows(q, 1 - c, 0, GROUP)], other.at[q], ps.at[q], pr.at[q], partner)

        @pl.when((r >= 1) & (r < NQ + 1))
        def _():
            q = r - 1

            @pl.when(q >= 4)
            def _():
                wait_bytes(other.at[q - 4, pl.ds(0, GROUP - BLOCK)], ss.at[q - 4])

            wait_bytes(other.at[q], pr.at[q])
            sums[sum_rows(q, 0), :] = pair_sum(q, z_far, BLOCK, 0).astype(BF16)
            remote(sums.at[sum_rows(q, 0, HALF)], far_lo.at[q], ss.at[q], rr_far_lo.at[q], up)
            remote(sums.at[sum_rows(q, 0, HALF, HALF)], far_hi.at[q], ss.at[q], rr_far_hi.at[q], dn)
            sums[sum_rows(q, 1), :] = pair_sum(q, z_up, BLOCK, 0).astype(BF16)
            remote(sums.at[sum_rows(q, 1, HALF, HALF)], ring_lo.at[q, upper], ss.at[q], rr_lo.at[q], up)
            sums[sum_rows(q, 2), :] = pair_sum(q, z_dn, BLOCK, 0).astype(BF16)
            remote(sums.at[sum_rows(q, 2, HALF)], ring_hi.at[q, lower], ss.at[q], rr_hi.at[q], dn)
            sums[sum_rows(q, 3), :] = pair_sum(q, z, BLOCK, 0).astype(BF16)

        @pl.when((r >= 2) & (r < NQ + 2))
        def _():
            q = r - 2
            wait_bytes(far_lo.at[q], rr_far_lo.at[q])
            rows = sum_rows(q, 1, HALF)
            sums[rows, :] = (sums[rows, :].astype(F32) + far_lo[q].astype(F32)).astype(BF16)
            remote(sums.at[rows], ring_lo.at[q, lower], ss.at[q], rr_lo.at[q], up)
            wait_bytes(far_hi.at[q], rr_far_hi.at[q])
            rows = sum_rows(q, 2, HALF, HALF)
            sums[rows, :] = (sums[rows, :].astype(F32) + far_hi[q].astype(F32)).astype(BF16)
            remote(sums.at[rows], ring_hi.at[q, upper], ss.at[q], rr_hi.at[q], dn)

        @pl.when((r >= 3) & (r < NQ + 3))
        def _():
            q = r - 3
            wait_bytes(ring_lo.at[q], rr_lo.at[q])
            wait_bytes(ring_hi.at[q], rr_hi.at[q])
            wait_packet_sends(q, fs)
            wait_bytes(gathered.at[q, pl.ds(0, 7)], ags.at[q])

            total = (
                sums[sum_rows(q, 3), :].astype(F32) + ring_lo[q].astype(F32) + ring_hi[q].astype(F32)
            ).astype(BF16)
            rows = jnp.concatenate([total[0:HALF], total[HALF:BLOCK]], axis=1)
            pack[q] = dot(expand[...], segments(rows)).astype(BF16)
            send_packets(q, back_at, ts, tr.at[q])

        @pl.when((r >= 4) & (r < NQ + 4))
        def _():
            q = r - 4
            slot = q % 2

            @pl.when(q >= 2)
            def _():
                fin_copy(q - 2, mixed_hbm).wait()

            wait_bytes(back.at[q], tr.at[q])

            @pl.when(q >= 1)
            def _():
                wait_packet_sends(q - 1, ts)

            def result(rows):
                done = dot(finish[...], rows).astype(BF16)
                st_fin[slot, :, 0:SEG] = done[0:TOKENS]
                st_fin[slot, :, SEG : 2 * SEG] = done[TOKENS : 2 * TOKENS]
                st_fin[slot, :, 2 * SEG : PAIR] = done[2 * TOKENS :, 0 : PAIR - 2 * SEG]

            @pl.when(q < NF)
            def _():
                rows = back[q]
                result((rows.astype(F32) * row_scale[:, 0:1]).astype(BF16))
                fin_copy(q, mixed_hbm).start()
                part = (lax.broadcasted_iota(jnp.int32, (PACK, TOKENS), 0) % PAD) // CAP
                scores[...] += jnp.where(
                    part == 0,
                    dot_nt(rows, cot[q, :, 0:SEG]),
                    jnp.where(
                        part == 1,
                        dot_nt(rows, cot[q, :, SEG : 2 * SEG]),
                        dot_nt(rows[:, 0 : PAIR - 2 * SEG], cot[q, :, 2 * SEG : PAIR]),
                    ),
                )

            @pl.when(q >= NF)
            def _():
                result(back[q])
                fin_copy(q, dtok_hbm).start()

            @pl.when(q == NF)
            def _():
                by_slot = chosen[...] * scores[...]
                for k in range(TOP):
                    hit = ids_ref[k : k + 1, :] == lax.broadcasted_iota(jnp.int32, (PACK, TOKENS), 0) // PAD
                    dw_ref[k : k + 1, :] = jnp.sum(jnp.where(hit, by_slot, 0.0), axis=0, keepdims=True)
                dw_copy.start()

        for h in range(2):

            @pl.when((t >= GRADS) & (t < GRADS + NF))
            def _():
                g = t - GRADS
                q = 2 * g + h

                @pl.when(q >= 2)
                def _():
                    for copy in grad_copies(q - 2):
                        copy.wait()

                dec = gathered[g, :, h * HALF : (h + 1) * HALF, :].reshape(ROWS, CW)
                grd = gathered[NF + g, :, h * HALF : (h + 1) * HALF, :].reshape(ROWS, CW)
                st_down[h] = dot(hid_t[...], grd).astype(BF16)
                st_wide[h] = dot(dpre_t[...], dec).T.astype(BF16)
                for copy in grad_copies(q):
                    copy.start()

    for q in (NQ - 2, NQ - 1):
        wait_bytes(other.at[q], ps.at[q])
        for copy in grad_copies(q) + (fin_copy(q, dtok_hbm),):
            copy.wait()
    for q in range(NQ - 4, NQ):
        wait_bytes(other.at[q, pl.ds(0, GROUP - BLOCK)], ss.at[q])

    wait_packet_sends(NQ - 1, ts)
    dw_copy.wait()


def copy_out(*refs):
    count = (len(refs) - 2) // 3
    sources, results, held = refs[:count], refs[count : 2 * count], refs[2 * count : 3 * count]
    in_sem, out_sem = refs[3 * count :]
    reads, writes = [], []
    for i in range(count):
        rows = held[i].shape[0] // PARTS
        for p in range(PARTS if rows >= 16 else 1):
            part = pl.ds(p * rows, rows) if rows >= 16 else pl.ds(0, held[i].shape[0])
            reads.append(pltpu.make_async_copy(sources[i].at[part], held[i].at[part], in_sem.at[i, p]))
            writes.append(pltpu.make_async_copy(held[i].at[part], results[i].at[part], out_sem.at[i, p]))
    for copy in reads:
        copy.start()
    for read, write in zip(reads, writes):
        read.wait()
        write.start()
    for copy in writes:
        copy.wait()


def on_device(tokens, expert_ids, route_weights, grad_out, gate_weight, up_weight, down_weight):
    any_spec = pl.BlockSpec(memory_space=pl.ANY)
    shape = jax.ShapeDtypeStruct
    dma = pltpu.SemaphoreType.DMA
    outs = (
        shape((TOKENS, D), BF16),
        shape((TOKENS, D), BF16),
        shape((TOP, TOKENS), F32),
        shape((D, HID), BF16),
        shape((D, HID), BF16),
        shape((HID, D), BF16),
    )
    results = pl.pallas_call(
        kernel,
        out_shape=outs,
        in_specs=[any_spec] * 7,
        out_specs=(any_spec,) * 6,
        scratch_shapes=[
            pltpu.VMEM((NQ, PACK, SEG), BF16),
            pltpu.VMEM((NQ, PACK, SEG), BF16),
            pltpu.VMEM((4 * GROUP, CW), BF16),
            pltpu.VMEM((NQ, 2 * NZ, BLOCK, CW), BF16),
            pltpu.VMEM((D, 2 * HID), BF16),
            pltpu.VMEM((NQ, HID, CW), BF16),
            pltpu.VMEM((NF, TOKENS, PAIR), BF16),
            pltpu.VMEM((4 * GROUP, CW), BF16),
            pltpu.VMEM((NQ, GROUP, CW), BF16),
            pltpu.VMEM((NQ, BLOCK, CW), BF16),
            pltpu.VMEM((NQ, BLOCK, CW), BF16),
            pltpu.VMEM((NQ, HALF, CW), BF16),
            pltpu.VMEM((NQ, HALF, CW), BF16),
            pltpu.VMEM((NQ, PACK, SEG), BF16),
            pltpu.VMEM((2, TOKENS, PAIR), BF16),
            pltpu.VMEM((2, HID, CW), BF16),
            pltpu.VMEM((2, CW, 2 * HID), BF16),
            pltpu.VMEM((TOP, TOKENS), jnp.int32),
            pltpu.VMEM((TOP, TOKENS), F32),
            pltpu.VMEM((TOP, TOKENS), F32),
            pltpu.VMEM((PACK, TOKENS), F32),
            pltpu.VMEM((PACK, SEGS * TOKENS), BF16),
            pltpu.VMEM((SEGS * TOKENS, PACK), BF16),
            pltpu.VMEM((SEGS * HALF, PACK), BF16),
            pltpu.VMEM((PACK, SEGS * HALF), BF16),
            pltpu.VMEM((PACK, 128), F32),
            pltpu.VMEM((ROWS, 2 * HID), F32),
            pltpu.VMEM((ROWS, HID), F32),
            pltpu.VMEM((ROWS, HID), BF16),
            pltpu.VMEM((ROWS, 2 * HID), BF16),
            pltpu.VMEM((HID, ROWS), BF16),
            pltpu.VMEM((2 * HID, ROWS), BF16),
            pltpu.VMEM((PACK, TOKENS), F32),
            dma((4, NQ)),
        ]
        + [dma((NQ,))] * 17
        + [dma((2,)), dma((3, 2))],
        compiler_params=pltpu.CompilerParams(
            collective_id=0, has_side_effects=True, vmem_limit_bytes=VMEM_LIMIT
        ),
        cost_estimate=pl.CostEstimate(
            flops=9 * 2 * ROWS * D * HID, bytes_accessed=10 * D * 256, transcendentals=ROWS * HID
        ),
        name="expert_layer",
    )(expert_ids.T, route_weights.T, tokens, grad_out, gate_weight, up_weight, down_weight)
    mixed, dtok, dw, dgate, dup, ddown = pl.pallas_call(
        copy_out,
        out_shape=outs,
        in_specs=[any_spec] * 6,
        out_specs=(any_spec,) * 6,
        scratch_shapes=[pltpu.VMEM(o.shape, o.dtype) for o in outs] + [dma((6, PARTS)), dma((6, PARTS))],
        compiler_params=pltpu.CompilerParams(vmem_limit_bytes=VMEM_LIMIT),
        name="copy_out",
    )(*results)
    return (mixed, dtok, dw.T, dgate, dup, ddown)


def solution(mesh):
    rows = P(("node", "local"), None)
    cols = P(None, ("node", "local"))
    return jax.shard_map(
        on_device,
        mesh=mesh,
        in_specs=(rows, rows, rows, rows, cols, cols, rows),
        out_specs=(rows, rows, rows, cols, cols, rows),
        check_vma=False,
    )
```

profile of v0, /device:TPU:0, one launch (start us, length us, event | category | flops | bytes accessed | tf_op | source)
XLA Modules:
  0.0 182.9 jit_solution(13195586955262351578)
XLA Ops:
  0.6 174.8 %expert_layer.1 = (bf16[128,7168]{1,0:T(8,128)(2,1)}, bf16[128,7168]{1,0:T(8,128)(2,1)}, f32[8,128]{1,0:T(8,128)}, bf16[7168,128]{1,0:T(8,128)(2,1)}, bf16[7168,...) custom-call(s32[8,128]{1,0:T(8,128)} %bitcast.3, f32[8,128]{1,0:T(8,128)} %bitcast.4, bf16[128,7168]{1,0:T(8,128)(2,1)} %tokens_hbm.1, ...), custom_call_target="tpu_custom_call" | custom-call | flops 10569646080 | bytes 18350080 | tf_op jit(solution)/shard_map/expert_layer/pallas_call | solution.py:608
  175.4 7.5 %copy_out.1 = (bf16[128,7168]{1,0:T(8,128)(2,1)}, bf16[128,7168]{1,0:T(8,128)(2,1)}, f32[8,128]{1,0:T(8,128)}, bf16[7168,128]{1,0:T(8,128)(2,1)}, bf16[7168,128]{1,0:T(8,128)(2,1)}, /*index=5*/bf16[128,7168]{1,0:T(8,128)(2,1)}) custom-call(bf16[128,7168]{1,0:T(8,128)(2,1)} %get-tuple-element.18.refs_0_, bf16[128,7168]{1,0:T(8,128)(2,1)} %get-tuple-element.19.refs_1_, ...), custom_call_target="tpu_custom_call" | custom-call | tf_op jit(solution)/shard_map/copy_out/pallas_call | solution.py:659
where the time goes:
time: 183 us
  Pallas kernels  182 us (99%)
    pallas_call x1, Pallas kernels, on_device(): pl.pallas_call(kernel, out_shape=outs, in_specs=[any_spec] * 7, out_specs...  175 us
    pallas_call x1, Pallas kernels, on_device(): pl.pallas_call(copy_out, out_shape=outs, in_specs=[any_spec] * 6, out_spe...  7.5 us

commit v1 on v0

--- a/solution.py
+++ b/solution.py
@@ -448,6 +448,18 @@
 
             remote(partial.at[partial_rows(q, 1 - c, 0, GROUP)], other.at[q], ps.at[q], pr.at[q], partner)
 
+        @pl.when((r >= 2) & (r < NQ + 2))
+        def _():
+            q = r - 2
+            wait_bytes(far_lo.at[q], rr_far_lo.at[q])
+            rows = sum_rows(q, 1, HALF)
+            sums[rows, :] = (sums[rows, :].astype(F32) + far_lo[q].astype(F32)).astype(BF16)
+            remote(sums.at[rows], ring_lo.at[q, lower], ss.at[q], rr_lo.at[q], up)
+            wait_bytes(far_hi.at[q], rr_far_hi.at[q])
+            rows = sum_rows(q, 2, HALF, HALF)
+            sums[rows, :] = (sums[rows, :].astype(F32) + far_hi[q].astype(F32)).astype(BF16)
+            remote(sums.at[rows], ring_hi.at[q, upper], ss.at[q], rr_hi.at[q], dn)
+
         @pl.when((r >= 1) & (r < NQ + 1))
         def _():
             q = r - 1
@@ -465,18 +477,6 @@
             sums[sum_rows(q, 2), :] = pair_sum(q, z_dn, BLOCK, 0).astype(BF16)
             remote(sums.at[sum_rows(q, 2, HALF)], ring_hi.at[q, lower], ss.at[q], rr_hi.at[q], dn)
             sums[sum_rows(q, 3), :] = pair_sum(q, z, BLOCK, 0).astype(BF16)
-
-        @pl.when((r >= 2) & (r < NQ + 2))
-        def _():
-            q = r - 2
-            wait_bytes(far_lo.at[q], rr_far_lo.at[q])
-            rows = sum_rows(q, 1, HALF)
-            sums[rows, :] = (sums[rows, :].astype(F32) + far_lo[q].astype(F32)).astype(BF16)
-            remote(sums.at[rows], ring_lo.at[q, lower], ss.at[q], rr_lo.at[q], up)
-            wait_bytes(far_hi.at[q], rr_far_hi.at[q])
-            rows = sum_rows(q, 2, HALF, HALF)
-            sums[rows, :] = (sums[rows, :].astype(F32) + far_hi[q].astype(F32)).astype(BF16)
-            remote(sums.at[rows], ring_hi.at[q, upper], ss.at[q], rr_hi.at[q], dn)
 
         @pl.when((r >= 3) & (r < NQ + 3))
         def _():

time: 183 us -> 188 us (1.027)
  Pallas kernels: 182 us -> 187 us
    pallas_call x1, Pallas kernels: 175 us -> 179 us  [on_device(): pl.pallas_call(kernel, out_shape=outs, in_specs=[any_spec] * 7, out_specs...]
where the time goes in v1:
time: 188 us; the launch traced here: 187 us
  Pallas kernels  187 us (99%)
    pallas_call x1, Pallas kernels, on_device(): pl.pallas_call(kernel, out_shape=outs, in_specs=[any_spec] * 7, out_specs...  179 us
    pallas_call x1, Pallas kernels, on_device(): pl.pallas_call(copy_out, out_shape=outs, in_specs=[any_spec] * 6, out_spe...  7.5 us

profile of v1, /device:TPU:0, one launch (start us, length us, event | category | flops | bytes accessed | tf_op | source)
XLA Modules:
  0.0 187.5 jit_solution(17875035688168456871)
XLA Ops:
  0.6 179.3 %expert_layer.1 = (bf16[128,7168]{1,0:T(8,128)(2,1)}, bf16[128,7168]{1,0:T(8,128)(2,1)}, f32[8,128]{1,0:T(8,128)}, bf16[7168,128]{1,0:T(8,128)(2,1)}, bf16[7168,...) custom-call(s32[8,128]{1,0:T(8,128)} %bitcast.3, f32[8,128]{1,0:T(8,128)} %bitcast.4, bf16[128,7168]{1,0:T(8,128)(2,1)} %tokens_hbm.1, ...), custom_call_target="tpu_custom_call" | custom-call | flops 10569646080 | bytes 18350080 | tf_op jit(solution)/shard_map/expert_layer/pallas_call | solution.py:608
  180.0 7.5 %copy_out.1 = (bf16[128,7168]{1,0:T(8,128)(2,1)}, bf16[128,7168]{1,0:T(8,128)(2,1)}, f32[8,128]{1,0:T(8,128)}, bf16[7168,128]{1,0:T(8,128)(2,1)}, bf16[7168,128]{1,0:T(8,128)(2,1)}, /*index=5*/bf16[128,7168]{1,0:T(8,128)(2,1)}) custom-call(bf16[128,7168]{1,0:T(8,128)(2,1)} %get-tuple-element.18.refs_0_, bf16[128,7168]{1,0:T(8,128)(2,1)} %get-tuple-element.19.refs_1_, ...), custom_call_target="tpu_custom_call" | custom-call | tf_op jit(solution)/shard_map/copy_out/pallas_call | solution.py:659
